TPU v7x, 256 devices: a whole 4x4x8 slice. The times are simulated.
256 devices in a mesh: tile: 64 (over z, y, core), frame: 4 (over x).
Axes of the slice: x: 4, y: 4, z: 8, core: 2. Of those that a mesh axis runs over, the one named last changes fastest.
Arguments:
- feats: bfloat16 [4, 16384, 256], P('frame', 'tile'), may hold values from -6 to 6
- routes: int32 [4, 64, 64], P('frame'), may hold values from 0 to 63, as said below
- interp: bfloat16 [4, 64, 16384, 128], P('frame', None, 'tile'), may hold values from -0.5 to 0.5
- w_value: bfloat16 [256, 256], replicated, may hold values from -0.375 to 0.375
- w_attn: bfloat16 [256, 64], replicated, may hold values from -48 to 48
- w_out: bfloat16 [256, 256], replicated, may hold values from -0.375 to 0.375
- grad_out: bfloat16 [4, 16384, 256], P('frame', 'tile'), may hold values from -6 to 6
Outputs:
- grad_feats: bfloat16 [4, 16384, 256], P('frame', 'tile')
- grad_w_value: float32 [256, 256], replicated
- grad_w_attn: float32 [256, 64], replicated
- grad_w_out: float32 [256, 256], replicated
Inputs may be any that keep to these rules, and one draw needn't show every extreme that they name: `routes`: within one frame a reader tile names any one owner tile in at most 2 of its 64 columns; in every frame some owner tile is named in exactly 2 columns by every reader tile.
All inputs are finite; a program needn't handle non-finite values.
Results may differ from a plain program's by a relative error of at most 0.022.
Values may be sent and summed in bfloat16 or wider, within the bound.
A program may use at most 128 MiB of HBM per device.

v0:
```python
import math
import jax
import jax.numpy as jnp
from jax import lax
from jax.sharding import PartitionSpec as P

H = 8
L = 2
P_SIZE = 4


def per_device(feats, routes, interp, w_value, w_attn, w_out, grad_out):
    inputs_now = feats[0]
    grads_now = grad_out[0]
    tile_weights = interp[0]
    routes_now = routes[0]
    tile_count = lax.axis_size("tile")
    myself = lax.axis_index("tile")
    row_count = inputs_now.shape[0]
    model_width = inputs_now.shape[1]
    column_count = tile_weights.shape[0]
    cell_count = tile_weights.shape[2]
    head_count = H
    level_count = L
    point_count = P_SIZE
    group_width = level_count * point_count
    head_dim = model_width // head_count
    capacity = max(2, 2 * column_count // tile_count)
    column = jnp.arange(column_count, dtype=jnp.int32)
    head_of = column // group_width
    level_of = column // point_count % level_count
    lookup_index = level_of * head_count + head_of
    my_routes = lax.dynamic_index_in_dim(routes_now, myself, 0, keepdims=False)
    earlier = (my_routes[None, :] == my_routes[:, None]) & (column[None, :] < column[:, None])
    ranking = jnp.sum(earlier.astype(jnp.int32), axis=1)
    slot_index = my_routes * capacity + ranking
    aimed = routes_now == myself
    ordering = jnp.cumsum(aimed.astype(jnp.int32), axis=1) - 1
    slot_range = jnp.arange(capacity, dtype=jnp.int32)
    picked = aimed[:, None, :] & (ordering[:, None, :] == slot_range[None, :, None])
    filled = jnp.any(picked, axis=2)
    chosen = jnp.sum(jnp.where(picked, lookup_index[None, None, :], 0), axis=2)
    values = jnp.dot(inputs_now, w_value, preferred_element_type=jnp.float32).astype(jnp.bfloat16)
    lookup = values.reshape(level_count, cell_count, head_count, head_dim).transpose(0, 2, 3, 1)
    lookup = lookup.reshape(level_count * head_count, head_dim, cell_count)
    empty = jnp.zeros((column_count, head_dim, cell_count), jnp.bfloat16)
    pieces = lax.all_gather(lookup[None], "tile", axis=0, tiled=True)
    owner_count = pieces.shape[0]
    inside = (my_routes >= 0) & (my_routes < owner_count)
    found = pieces[jnp.clip(my_routes, 0, owner_count - 1), lookup_index]
    fetched = jnp.where(inside[:, None, None], found, empty)
    sampled = jnp.einsum("jdc,jqc->jdq", fetched, tile_weights, preferred_element_type=jnp.float32)
    logits = jnp.dot(inputs_now, w_attn, preferred_element_type=jnp.float32)
    attn = jax.nn.softmax(logits.reshape(row_count, head_count, group_width), axis=-1).reshape(
        row_count, column_count
    )
    attn_heads = attn.T.reshape(head_count, group_width, 1, row_count)
    sampled_heads = sampled.reshape(head_count, group_width, head_dim, row_count)
    mixed = (
        jnp.sum(attn_heads * sampled_heads, axis=1)
        .reshape(model_width, row_count)
        .T.astype(jnp.bfloat16)
    )
    grad_mixed = jnp.dot(grads_now, w_out.T, preferred_element_type=jnp.float32)
    grad_mixed_heads = grad_mixed.T.reshape(head_count, 1, head_dim, row_count)
    grad_attn = jnp.sum(grad_mixed_heads * sampled_heads, axis=2).reshape(column_count, row_count).T
    grad_attn = grad_attn.reshape(row_count, head_count, group_width)
    attn_query = attn.reshape(row_count, head_count, group_width)
    inner_term = jnp.sum(attn_query * grad_attn, axis=-1, keepdims=True)
    grad_logits = (
        (attn_query * (grad_attn - inner_term))
        .reshape(row_count, column_count)
        .astype(jnp.bfloat16)
    )
    grad_sampled = (
        (attn_heads * grad_mixed_heads)
        .reshape(column_count, head_dim, row_count)
        .astype(jnp.bfloat16)
    )
    contrib = jnp.einsum(
        "jdq,jqc->jdc", grad_sampled, tile_weights, preferred_element_type=jnp.float32
    )
    outgoing = (
        jnp.zeros((tile_count * capacity, head_dim, cell_count), jnp.float32)
        .at[slot_index]
        .set(contrib)
    )
    returned = lax.all_to_all(
        outgoing.reshape(tile_count, capacity, head_dim, cell_count).astype(jnp.bfloat16),
        "tile",
        split_axis=0,
        concat_axis=0,
        tiled=True,
    ).astype(jnp.float32)
    table_range = jnp.arange(level_count * head_count, dtype=jnp.int32)
    member = (chosen.reshape(-1)[None, :] == table_range[:, None]) & filled.reshape(-1)[None, :]
    grad_lookup = jnp.dot(
        member.astype(jnp.float32),
        returned.reshape(tile_count * capacity, head_dim * cell_count),
        precision=lax.Precision.HIGHEST,
    )
    grad_values = grad_lookup.reshape(level_count, head_count, head_dim, cell_count).transpose(
        0, 3, 1, 2
    )
    grad_values = grad_values.reshape(row_count, model_width).astype(jnp.bfloat16)
    grad_query = jnp.dot(grad_logits, w_attn.T, preferred_element_type=jnp.float32)
    part_attn = jnp.dot(inputs_now.T, grad_logits, preferred_element_type=jnp.float32)
    part_out = jnp.dot(mixed.T, grads_now, preferred_element_type=jnp.float32)
    grad_inputs = grad_query + jnp.dot(grad_values, w_value.T, preferred_element_type=jnp.float32)
    part_value = jnp.dot(inputs_now.T, grad_values, preferred_element_type=jnp.float32)
    totals = lax.psum((part_value, part_attn, part_out), ("tile", "frame"))
    factor = 1.0 / math.sqrt(tile_count * lax.axis_size("frame") * row_count)
    return (
        grad_inputs.astype(jnp.bfloat16)[None],
        totals[0] * factor,
        totals[1] * factor,
        totals[2] * factor,
    )


def solution(mesh):
    in_specs = (
        P("frame", "tile", None),
        P("frame", None, None),
        P("frame", None, "tile", None),
        P(),
        P(),
        P(),
        P("frame", "tile", None),
    )
    out_specs = (P("frame", "tile", None), P(), P(), P())
    return jax.shard_map(
        per_device, mesh=mesh, in_specs=in_specs, out_specs=out_specs, check_vma=False
    )
```

profile of v0, /device:TPU:1, one launch (start us, length us, event | category | flops | bytes accessed | tf_op | source)
XLA Modules:
  0.0 408.1 jit_solution(1071865935539580949)
XLA Ops:
  7.2 0.8 copy-done
  8.1 1.1 convolution_convert_fusion
  9.3 0.7 copy.29
  10.0 0.7 compare_and_fusion
  10.7 0.2 convert_reduce_fusion
  10.9 1.0 fusion.13
  11.9 1.2 fusion.25
  13.1 85.5 %all-gather.2.cloned.1.call-done = bf16[64,16,32,128]{3,2,1,0:T(8,128)(2,1)} async-done(((bf16[1,16,32,128]{3,2,1,0:T(8,128)(2,1)}), bf16[64,16,32,128]{3,2,1,0:T(8,128)(2,1)}) %all-gather.2.cloned.1.call-update) | async-done | bytes 8388624 | tf_op jit(solution)/shard_map/all_gather | solution.py:47
  98.7 4.1 %gather_fusion = bf16[64,32,128]{2,1,0:T(8,128)(2,1)S(1)} fusion(bf16[64,16,32,128]{3,2,1,0:T(8,128)(2,1)} %all-gather.2.cloned.1.call-done, s32[64]{0:T(128)S(1)} %get-tuple-element.30), kind=kCustom, calls=%fused_computation | custom fusion | bytes 1049088 | tf_op jit(solution)/shard_map/gather | solution.py:50
  102.8 5.2 %fusion.8 = (bf16[64,32,256]{2,1,0:T(8,128)(2,1)S(1)}, f32[64,256]{1,0:T(8,128)S(1)}, f32[64,32,256]{2,1,0:T(8,128)}) fusion(f32[64,256]{1,0:T(8,128)S(1)} %bitcast.145, f32[8,32,256]{2,1,0:T(8,128)S(1)} %fusion.25, bf16[1,64,256,128]{3,2,1,0:T(8,128)(2,1)} %param.9, bf16[64,32,128]{2,1,0:T(8,128)(2,1)S(1)} %gather_fusion, ...), kind=kOutput, calls=%fused_computation.12 | convolution fusion | flops 136560640 | bytes 8257600 | tf_op jit(solution)/shard_map/jdc,jqc->jdq/dot_general | solution.py:52
  108.0 0.7 fusion.3
  108.7 0.3 broadcast_in_dim.30
  109.0 2.5 scatter_fusion
  111.5 1.2 convert_element_type.58
  112.7 6.4 %all-to-all-start = ((bf16[64,2,32,128]{3,2,1,0:T(8,128)(2,1)}), bf16[64,2,32,128]{3,2,1,0:T(8,128)(2,1)S(1)}, u32[]{:S(2)}, u32[]{:S(2)}) async-start(bf16[64,2,32,128]{3,2,1,0:T(8,128)(2,1)} %bitcast.26), calls=%async_computation | async-start | bytes 2097152 | tf_op jit(solution)/shard_map/all_to_all | solution.py:88
  119.2 0.2 reduce_window_sum.11
  120.2 0.3 multiply_reduce_fusion
  120.5 0.8 convolution_bitcast_fusion.1
  121.3 1.8 fusion.27
  123.1 24.0 %all-to-all-done = bf16[64,2,32,128]{3,2,1,0:T(8,128)(2,1)S(1)} async-done(((bf16[64,2,32,128]{3,2,1,0:T(8,128)(2,1)}), bf16[64,2,32,128]{3,2,1,0:T(8,128)(2,1)S(1)}, u32[]{:S(2)}, u32[]{:S(2)}) %all-to-all-start) | async-done | bytes 1048608 | tf_op jit(solution)/shard_map/all_to_all | solution.py:88
  147.1 0.5 copy.50
  147.5 0.7 copy.32
  148.2 0.4 fusion.11
  148.6 0.2 copy.33
  148.8 0.9 convolution_bitcast_fusion
  149.7 0.2 fusion.19
  150.0 0.9 fusion.10
  150.8 247.0 %all-reduce.3.cloned.1.call-done = (f32[256,256]{0,1:T(8,128)}, f32[256,64]{0,1:T(8,128)}, f32[256,256]{0,1:T(8,128)}) async-done(((f32[256,256]{0,1:T(8,128)}, f32[256,64]{0,1:T(8,128)}, f32[256,256]{0,1:T(8,128)}), (f32[256,256]{0,1:T(8,128)}, f32[256,64]{0,1:T(8,128)}, f32[256,256]{0,1:T(8,128)})) %all-reduce.3.cloned.1.call-update) | async-done | bytes 589840 | tf_op jit(solution)/shard_map/psum | solution.py:111
  397.8 1.1 broadcast_multiply_fusion
  398.9 0.8 copy.35
  399.8 0.8 copy.36
  400.6 0.6 broadcast_multiply_fusion.2
  (30 shorter events, 1.1 us)
Async XLA Ops:
  7.2 0.9 copy-start
  7.2 91.5 %all-gather.2.cloned.1.call-start = ((), (), s32[]{:S(2)}) async-start(), calls=%async_computation.1 | async-start | bytes 8519680 | tf_op jit(solution)/shard_map/all_gather | solution.py:47
  102.8 5.3 %copy-start.1 = (bf16[1,64,256,128]{3,2,1,0:T(8,128)(2,1)S(1)}, bf16[1,64,256,128]{3,2,1,0:T(8,128)(2,1)}, u32[]{:S(2)}) copy-start(bf16[1,64,256,128]{3,2,1,0:T(8,128)(2,1)} %param.9) | copy-start | bytes 12582916
  111.5 7.6 %copy-start.5 = (s32[1,64,64]{2,1,0:T(8,128)S(1)}, s32[1,64,64]{2,1,0:T(8,128)}, u32[]{:S(2)}) copy-start(s32[1,64,64]{2,1,0:T(8,128)} %param.8) | copy-start | bytes 49156
  112.7 7.5 %copy-start.2 = (f32[64,32,256]{2,1,0:T(8,128)S(1)}, f32[64,32,256]{2,1,0:T(8,128)}, u32[]{:S(2)}) copy-start(f32[64,32,256]{2,1,0:T(8,128)} %get-tuple-element.31) | copy-start | bytes 6291460
  112.7 34.4 %all-to-all-start = ((bf16[64,2,32,128]{3,2,1,0:T(8,128)(2,1)}), bf16[64,2,32,128]{3,2,1,0:T(8,128)(2,1)S(1)}, u32[]{:S(2)}, u32[]{:S(2)}) async-start(bf16[64,2,32,128]{3,2,1,0:T(8,128)(2,1)} %bitcast.26), calls=%async_computation | async-start | bytes 2097152 | tf_op jit(solution)/shard_map/all_to_all | solution.py:88
  119.1 278.7 %all-reduce.3.cloned.1.call-start = ((), (), s32[]{:S(2)}) async-start(), calls=%async_computation.2 | async-start | bytes 1179648 | tf_op jit(solution)/shard_map/psum | solution.py:111
  147.5 2.2 copy-start.6
  147.5 2.4 copy-start.3
  397.8 2.8 copy-start.4
Sparse Core Ops, SparseCore 0:
  11.4 87.2 all-gather.1
  149.8 247.9 all-reduce.2
where the time goes:
time: 408 us
  waiting for transfers between devices  357 us (88%)
  between operations  14.3 us (4%)
  matrix products  14.2 us (3%)
  local copies, waits for them, and re-layouts  12 us (3%)
  starting transfers between devices  6.44 us (2%)
  other arithmetic  4.6 us (1%)
    psum x1, waiting for transfers between devices, per_device(): totals = lax.psum((part_value, part_attn, part_out), ('tile', 'frame'))  247 us
    all_gather x1, waiting for transfers between devices, per_device(): pieces = lax.all_gather(lookup[None], 'tile', axis=0, tiled=True)  85.5 us
    all_to_all x1, waiting for transfers between devices, per_device(): lax.all_to_all(outgoing.reshape(tile_count, capacity, head_dim, cell_coun...  24 us
  transfers between devices with their start and end apart: 3, of which 3 were waited for; matrix products, arithmetic and copies ran while one was open for 2% of the time, Pallas kernels for 0%

commit v1 on v0

--- a/solution.py
+++ b/solution.py
@@ -108,7 +108,7 @@
     part_out = jnp.dot(mixed.T, grads_now, preferred_element_type=jnp.float32)
     grad_inputs = grad_query + jnp.dot(grad_values, w_value.T, preferred_element_type=jnp.float32)
     part_value = jnp.dot(inputs_now.T, grad_values, preferred_element_type=jnp.float32)
-    totals = lax.psum((part_value, part_attn, part_out), ("tile", "frame"))
+    totals = lax.psum(lax.psum((part_value, part_attn, part_out), "tile"), "frame")
     factor = 1.0 / math.sqrt(tile_count * lax.axis_size("frame") * row_count)
     return (
         grad_inputs.astype(jnp.bfloat16)[None],

time: 408 us -> 389 us (0.953)
  waiting for transfers between devices: 357 us -> 336 us
    psum x1 -> x2, waiting for transfers between devices: 247 us -> 227 us  [the longest x1 179 us: per_device(): lax.psum((part_value, part_attn, part_out), 'tile')]
  transfers between devices with their start and end apart: 3 -> 4, of which waited for: 3 -> 4; matrix products, arithmetic and copies ran while one was open for 2% -> 2% of each run, Pallas kernels for 0% -> 0%
where the time goes in v1:
time: 389 us; the launch traced here: 388 us
  waiting for transfers between devices  336 us (86%)
  matrix products  14.2 us (4%)
  between operations  14 us (4%)
  local copies, waits for them, and re-layouts  12 us (3%)
  starting transfers between devices  6.48 us (2%)
  other arithmetic  4.6 us (1%)
    psum x1, waiting for transfers between devices, per_device(): lax.psum((part_value, part_attn, part_out), 'tile')  179 us
    all_gather x1, waiting for transfers between devices, per_device(): pieces = lax.all_gather(lookup[None], 'tile', axis=0, tiled=True)  85.5 us
    psum x1, waiting for transfers between devices, per_device(): lax.psum(lax.psum((part_value, part_attn, part_out), 'tile'), 'frame')  48.2 us
    all_to_all x1, waiting for transfers between devices, per_device(): lax.all_to_all(outgoing.reshape(tile_count, capacity, head_dim, cell_coun...  24 us
  transfers between devices with their start and end apart: 4, of which 4 were waited for; matrix products, arithmetic and copies ran while one was open for 2% of the time, Pallas kernels for 0%

profile of v1, /device:TPU:1, one launch (start us, length us, event | category | flops | bytes accessed | tf_op | source)
XLA Modules:
  0.0 387.8 jit_solution(738270553978985553)
XLA Ops:
  7.2 0.8 copy-done
  8.1 1.1 convolution_convert_fusion
  9.3 0.7 copy.29
  10.0 0.7 compare_and_fusion
  10.7 0.2 convert_reduce_fusion
  10.9 1.0 fusion.13
  11.9 1.2 fusion.25
  13.1 85.5 %all-gather.2.cloned.1.call-done = bf16[64,16,32,128]{3,2,1,0:T(8,128)(2,1)} async-done(((bf16[1,16,32,128]{3,2,1,0:T(8,128)(2,1)}), bf16[64,16,32,128]{3,2,1,0:T(8,128)(2,1)}) %all-gather.2.cloned.1.call-update) | async-done | bytes 8388624 | tf_op jit(solution)/shard_map/all_gather | solution.py:47
  98.7 4.1 %gather_fusion = bf16[64,32,128]{2,1,0:T(8,128)(2,1)S(1)} fusion(bf16[64,16,32,128]{3,2,1,0:T(8,128)(2,1)} %all-gather.2.cloned.1.call-done, s32[64]{0:T(128)S(1)} %get-tuple-element.33), kind=kCustom, calls=%fused_computation | custom fusion | bytes 1049088 | tf_op jit(solution)/shard_map/gather | solution.py:50
  102.8 5.2 %fusion.8 = (bf16[64,32,256]{2,1,0:T(8,128)(2,1)S(1)}, f32[64,256]{1,0:T(8,128)S(1)}, f32[64,32,256]{2,1,0:T(8,128)}) fusion(f32[64,256]{1,0:T(8,128)S(1)} %bitcast.145, f32[8,32,256]{2,1,0:T(8,128)S(1)} %fusion.25, bf16[1,64,256,128]{3,2,1,0:T(8,128)(2,1)} %param.9, bf16[64,32,128]{2,1,0:T(8,128)(2,1)S(1)} %gather_fusion, ...), kind=kOutput, calls=%fused_computation.12 | convolution fusion | flops 136560640 | bytes 8257600 | tf_op jit(solution)/shard_map/jdc,jqc->jdq/dot_general | solution.py:52
  108.0 0.7 fusion.3
  108.7 0.3 broadcast_in_dim.30
  109.0 2.5 scatter_fusion
  111.5 1.2 convert_element_type.58
  112.7 6.4 %all-to-all-start = ((bf16[64,2,32,128]{3,2,1,0:T(8,128)(2,1)}), bf16[64,2,32,128]{3,2,1,0:T(8,128)(2,1)S(1)}, u32[]{:S(2)}, u32[]{:S(2)}) async-start(bf16[64,2,32,128]{3,2,1,0:T(8,128)(2,1)} %bitcast.26), calls=%async_computation | async-start | bytes 2097152 | tf_op jit(solution)/shard_map/all_to_all | solution.py:88
  119.2 0.2 reduce_window_sum.11
  120.2 0.3 multiply_reduce_fusion
  120.5 0.8 convolution_bitcast_fusion.1
  121.3 1.8 fusion.27
  123.1 24.0 %all-to-all-done = bf16[64,2,32,128]{3,2,1,0:T(8,128)(2,1)S(1)} async-done(((bf16[64,2,32,128]{3,2,1,0:T(8,128)(2,1)}), bf16[64,2,32,128]{3,2,1,0:T(8,128)(2,1)S(1)}, u32[]{:S(2)}, u32[]{:S(2)}) %all-to-all-start) | async-done | bytes 1048608 | tf_op jit(solution)/shard_map/all_to_all | solution.py:88
  147.1 0.5 copy.50
  147.5 0.7 copy.32
  148.2 0.4 fusion.11
  148.8 0.9 convolution_bitcast_fusion
  149.8 178.7 %all-reduce.5.cloned.1.call-done = (f32[256,256]{0,1:T(8,128)}, f32[256,64]{0,1:T(8,128)}, f32[256,256]{0,1:T(8,128)}) async-done(((f32[256,256]{0,1:T(8,128)}, f32[256,64]{0,1:T(8,128)}, f32[256,256]{0,1:T(8,128)}), (f32[256,256]{0,1:T(8,128)}, f32[256,64]{0,1:T(8,128)}, f32[256,256]{0,1:T(8,128)})) %all-reduce.5.cloned.1.call-update) | async-done | bytes 589840 | tf_op jit(solution)/shard_map/psum | solution.py:111
  328.4 0.2 fusion.19
  328.7 0.9 fusion.10
  329.6 48.2 %all-reduce.7.cloned.1.call-done = (f32[256,256]{0,1:T(8,128)}, f32[256,64]{0,1:T(8,128)}, f32[256,256]{0,1:T(8,128)}) async-done(((f32[256,256]{0,1:T(8,128)}, f32[256,64]{0,1:T(8,128)}, f32[256,256]{0,1:T(8,128)}), (f32[256,256]{0,1:T(8,128)}, f32[256,64]{0,1:T(8,128)}, f32[256,256]{0,1:T(8,128)})) %all-reduce.7.cloned.1.call-update) | async-done | bytes 589840 | tf_op jit(solution)/shard_map/psum | solution.py:111
  377.8 1.1 broadcast_multiply_fusion
  378.9 0.8 copy.35
  379.8 0.8 copy.36
  380.6 0.6 broadcast_multiply_fusion.2
  (33 shorter events, 1.3 us)
Async XLA Ops:
  7.2 0.9 copy-start
  7.2 91.5 %all-gather.2.cloned.1.call-start = ((), (), s32[]{:S(2)}) async-start(), calls=%async_computation.1 | async-start | bytes 8519680 | tf_op jit(solution)/shard_map/all_gather | solution.py:47
  102.8 5.3 %copy-start.1 = (bf16[1,64,256,128]{3,2,1,0:T(8,128)(2,1)S(1)}, bf16[1,64,256,128]{3,2,1,0:T(8,128)(2,1)}, u32[]{:S(2)}) copy-start(bf16[1,64,256,128]{3,2,1,0:T(8,128)(2,1)} %param.9) | copy-start | bytes 12582916
  111.5 7.6 %copy-start.5 = (s32[1,64,64]{2,1,0:T(8,128)S(1)}, s32[1,64,64]{2,1,0:T(8,128)}, u32[]{:S(2)}) copy-start(s32[1,64,64]{2,1,0:T(8,128)} %param.8) | copy-start | bytes 49156
  112.7 7.5 %copy-start.2 = (f32[64,32,256]{2,1,0:T(8,128)S(1)}, f32[64,32,256]{2,1,0:T(8,128)}, u32[]{:S(2)}) copy-start(f32[64,32,256]{2,1,0:T(8,128)} %get-tuple-element.34) | copy-start | bytes 6291460
  112.7 34.4 %all-to-all-start = ((bf16[64,2,32,128]{3,2,1,0:T(8,128)(2,1)}), bf16[64,2,32,128]{3,2,1,0:T(8,128)(2,1)S(1)}, u32[]{:S(2)}, u32[]{:S(2)}) async-start(bf16[64,2,32,128]{3,2,1,0:T(8,128)(2,1)} %bitcast.26), calls=%async_computation | async-start | bytes 2097152 | tf_op jit(solution)/shard_map/all_to_all | solution.py:88
  119.1 209.3 %all-reduce.5.cloned.1.call-start = ((), (), s32[]{:S(2)}) async-start(), calls=%async_computation.2 | async-start | bytes 1179648 | tf_op jit(solution)/shard_map/psum | solution.py:111
  148.2 180.2 %copy-start.6 = (bf16[256,64]{0,1:T(8,128)(2,1)S(1)}, bf16[256,64]{0,1:T(8,128)(2,1)}, u32[]{:S(2)}) copy-start(bf16[256,64]{0,1:T(8,128)(2,1)} %param.11) | copy-start | bytes 98308
  148.2 180.5 %copy-start.3 = (bf16[256,256]{1,0:T(8,128)(2,1)S(1)}, bf16[256,256]{1,0:T(8,128)(2,1)}, u32[]{:S(2)}) copy-start(bf16[256,256]{1,0:T(8,128)(2,1)} %param.10) | copy-start | bytes 393220
  149.7 228.1 %all-reduce.7.cloned.1.call-start = ((), (), s32[]{:S(2)}) async-start(), calls=%async_computation.3 | async-start | bytes 1179648 | tf_op jit(solution)/shard_map/psum | solution.py:111
  377.8 2.8 copy-start.4
Sparse Core Ops, SparseCore 0:
  11.4 87.2 all-gather.1
  149.8 178.5 all-reduce.4
  330.9 46.8 all-reduce.6
